TPU v7x, 32 devices: a whole 2x2x4 slice. The times are simulated.
32 devices in a mesh: grp: 4 (over y, x), shard: 8 (over z, core).
Axes of the slice: x: 2, y: 2, z: 4, core: 2. Of those that a mesh axis runs over, the one named last changes fastest.
Arguments:
- src: float32 [512, 1024], P(('grp', 'shard')), may hold values from -64 to 64
- inv_src: float32 [512], P(('grp', 'shard')), may hold values from 5 to 250
- tgt: float32 [4096, 1024], P(('shard', 'grp')), may hold values from -64 to 64
- inv_tgt: float32 [4096], P(('shard', 'grp')), may hold values from 5 to 250
Outputs:
- margin: float32 [512, 4096], P('grp', 'shard')
All inputs are finite; a program needn't handle non-finite values.
Results may differ from a plain program's by a relative error of at most 0.00013.
Values sent between devices are 32-bit elements; how exact they have to be, the bound alone decides.
A program may use at most 64 MiB of HBM per device.

v0:
```python
import math

import jax
import jax.numpy as jnp
from jax import lax
from jax.sharding import PartitionSpec as P


def merged(part, axis, combine):
    gathered = jax.tree.map(lambda a: lax.all_gather(a, axis), part)

    def take(source):
        return jax.tree.map(lambda a: lax.dynamic_index_in_dim(a, source, 0, False), gathered)

    return lax.fori_loop(
        1, lax.axis_size(axis), lambda source, state: combine(state, take(source)), take(0)
    )


def unit_rows(rows):
    return rows * lax.rsqrt(jnp.sum(rows * rows, axis=1, keepdims=True) + 1e-06)


def combine(first, second):
    top = jnp.maximum(first[0], second[0])
    total = first[1] * jnp.exp(first[0] - top) + second[1] * jnp.exp(second[0] - top)
    return (top, total)


def tile_stats(logits, axis):
    top = jnp.max(logits, axis=axis)
    total = jnp.sum(jnp.exp(logits - jnp.expand_dims(top, axis)), axis=axis)
    return (top, total)


def products(left, right):
    return jnp.dot(
        left, right.T, precision=lax.Precision.HIGHEST, preferred_element_type=jnp.float32
    )


def merge_rows(row_max, row_sum):
    return merged((row_max, row_sum), "shard", combine)


def body(src, inv_src, tgt, inv_tgt):
    groups = lax.axis_size("grp")
    shards = lax.axis_size("shard")
    src_unit = unit_rows(src)
    tgt_unit = unit_rows(tgt)
    width = tgt.shape[0]
    height = src.shape[0] * shards
    cols_all, inv_all = (
        lax.all_gather(tgt_unit, "grp", axis=0, tiled=True),
        lax.all_gather(inv_tgt, "grp", axis=0, tiled=True),
    )
    columns = cols_all.shape[0]
    col_max = jnp.full((columns,), -1e30, jnp.float32)
    col_sum = jnp.zeros((columns,), jnp.float32)
    rows = lax.all_gather(src_unit, "shard", axis=0, tiled=True)
    inv_piece = lax.all_gather(inv_src, "shard", axis=0, tiled=True)
    sims = products(rows, cols_all)
    inv_rows = inv_piece
    piece_max, piece_sum = tile_stats(sims * inv_piece[:, None], 1)
    row_max = piece_max
    row_sum = piece_sum
    col_max, col_sum = combine((col_max, col_sum), tile_stats(sims * inv_all[None, :], 0))
    sims_all, inv_rows, row_max, row_sum, col_max, col_sum = (
        sims,
        inv_rows,
        row_max,
        row_sum,
        col_max,
        col_sum,
    )
    col_max, col_sum = merged((col_max, col_sum), "grp", combine)
    col_all = col_max + jnp.log(col_sum) - math.log(height * groups)
    row_max, row_sum = merge_rows(row_max, row_sum)
    row_lse = row_max + jnp.log(row_sum) - math.log(groups * width * shards)
    scale = 0.5 * (inv_rows[:, None] + inv_all[None, :])
    return sims_all * scale - (jnp.logaddexp(row_lse[:, None], col_all[None, :]) - math.log(2.0))


def solution(mesh):
    return jax.shard_map(
        body,
        mesh=mesh,
        in_specs=(
            P(("grp", "shard"), None),
            P(("grp", "shard")),
            P(("shard", "grp"), None),
            P(("shard", "grp")),
        ),
        out_specs=P("grp", "shard"),
        check_vma=False,
    )
```

profile of v0, /device:TPU:0, one launch (start us, length us, event | category | flops | bytes accessed | tf_op | source)
XLA Modules:
  0.0 96.7 jit_solution(16064081526351136043)
XLA Ops:
  6.5 0.0 copy-start.3
  6.5 0.0 copy-start.2
  6.5 0.0 copy-start.1
  6.5 0.0 copy-start
  6.5 0.0 all-gather.9.cloned.1.call-start
  6.6 1.2 %multiply_reduce_fusion = f32[128]{0:T(128)S(1)} fusion(f32[128,1024]{1,0:T(8,128)} %param.10), kind=kLoop, calls=%fused_computation.9 | loop fusion | flops 262016 | bytes 524800 | tf_op jit(solution)/shard_map/reduce_sum | solution.py:21
  7.8 2.0 %broadcast_multiply_fusion = f32[128,1024]{1,0:T(8,128)} fusion(f32[128,1024]{1,0:T(8,128)} %param.10, f32[128]{0:T(128)S(1)} %add_rsqrt_fusion), kind=kLoop, calls=%fused_computation.21 | loop fusion | flops 131072 | bytes 1049088 | tf_op jit(solution)/shard_map/mul | solution.py:21
  9.7 0.0 all-gather.9.cloned.1.call-update
  9.8 0.0 copy-done.3
  9.8 0.6 dynamic-slice
  11.0 0.0 copy-done.2
  11.0 0.2 dynamic-update-slice
  11.3 0.0 copy-done.1
  11.3 9.4 %all-gather.2 = f32[4,1,128]{2,1,0:T(1,128)S(1)} all-gather(f32[1,1,128]{2,1,0:T(1,128)S(1)} %bitcast.62), channel_id=1, replica_groups=mesh['grp'=4,'shard'=8] {'grp'}, dimensions={0}, use_global_device_ids=true | all-gather | bytes 2560 | tf_op jit(solution)/shard_map/all_gather | solution.py:55
  20.6 14.6 %all-reduce = f32[128]{0:T(128)S(1)} all-reduce(f32[128]{0:T(128)S(1)} %dynamic-update-slice), channel_id=1, replica_groups=mesh['grp'=4,'shard'=8] {'shard'}, use_global_device_ids=true, to_apply=%add | all-reduce | flops 128 | bytes 1024
  35.3 0.0 copy-done
  35.3 0.1 multiply_reduce_fusion.3
  35.4 0.1 broadcast_multiply_fusion.1
  35.5 14.9 %all_gather.32 = f32[128,1024]{1,0:T(8,128)S(1)} all-gather(f32[16,1024]{1,0:T(8,128)S(1)} %broadcast_multiply_fusion.1), channel_id=1, replica_groups=mesh['grp'=4,'shard'=8] {'shard'}, dimensions={0}, use_global_device_ids=true | all-gather | bytes 589824 | tf_op jit(solution)/shard_map/all_gather | solution.py:60
  50.4 0.0 all-gather.9.cloned.1.call-done
  50.4 3.9 %multiply_reduce_fusion.2 = (f32[128]{0:T(128)S(1)}, f32[512]{0:T(512)S(1)}, f32[128,512]{1,0:T(8,128)S(1)}) fusion(f32[128]{0:T(128)S(1)} %all-reduce, f32[512]{0:T(512)S(1)} %bitcast.53, f32[128,1024]{1,0:T(8,128)S(1)} %all_gather.32, f32[512,1024]{1,0:T(8,128)} %all-gather.9.cloned.1.call-done), kind=kOutput, calls=%fused_computation.23 | convolution fusion | flops 805567872 | bytes 2888704 | tf_op jit(solution)/shard_map/dot_general | solution.py:37
  54.3 0.2 exponential_reduce_fusion.1
  54.5 8.0 %all-gather.5 = f32[4,1,512]{2,1,0:T(1,128)S(1)} all-gather(f32[1,1,512]{2,1,0:T(1,128)S(1)} %get-tuple-element.306), channel_id=1, replica_groups=mesh['grp'=4,'shard'=8] {'grp'}, dimensions={0}, use_global_device_ids=true | all-gather | bytes 10240 | tf_op jit(solution)/shard_map/all_gather | solution.py:10
  62.6 7.1 %all-gather.6 = f32[4,1,512]{2,1,0:T(1,128)S(1)} all-gather(f32[1,1,512]{2,1,0:T(1,128)S(1)} %get-tuple-element.305), channel_id=1, replica_groups=mesh['grp'=4,'shard'=8] {'grp'}, dimensions={0}, use_global_device_ids=true | all-gather | bytes 10240 | tf_op jit(solution)/shard_map/all_gather | solution.py:10
  69.7 9.2 %all-gather.4 = f32[8,1,128]{2,1,0:T(1,128)S(1)} all-gather(f32[1,1,128]{2,1,0:T(1,128)S(1)} %bitcast.61), channel_id=3, replica_groups=mesh['grp'=4,'shard'=8] {'shard'}, dimensions={0}, use_global_device_ids=true | all-gather | bytes 4608 | tf_op jit(solution)/shard_map/all_gather | solution.py:10
  78.9 9.5 %all-gather.3 = f32[8,1,128]{2,1,0:T(1,128)S(1)} all-gather(f32[1,1,128]{2,1,0:T(1,128)S(1)} %bitcast.60), channel_id=2, replica_groups=mesh['grp'=4,'shard'=8] {'shard'}, dimensions={0}, use_global_device_ids=true | all-gather | bytes 4608 | tf_op jit(solution)/shard_map/all_gather | solution.py:10
  88.4 0.3 while.34
  88.7 0.2 while.35
  88.9 1.0 %fusion.8 = f32[128,512]{1,0:T(8,128)} fusion(f32[128,512]{1,0:T(8,128)S(1)} %get-tuple-element.307, f32[512]{0:T(512)S(1)} %add_add_fusion, f32[128]{0:T(128)S(1)} %add_add_fusion.1, f32[512]{0:T(512)S(1)} %bitcast.55, f32[128]{0:T(128)S(1)} %all-reduce), kind=kLoop, calls=%fused_computation.18 | loop fusion | flops 851968 | bytes 529408 | tf_op jit(solution)/shard_map/sub | solution.py:81
  (25 shorter events, 0.3 us)
Async XLA Ops:
  6.5 3.2 %copy-start.3 = (u32[32]{0:T(128)S(1)}, u32[32]{0:T(128)}, u32[]{:S(2)}) copy-start(u32[32]{0:T(128)} %constant.115) | copy-start | bytes 388
  6.5 4.5 %copy-start.2 = (f32[16]{0:T(128)S(1)}, f32[16]{0:T(128)}, u32[]{:S(2)}) copy-start(f32[16]{0:T(128)} %param.9) | copy-start | bytes 196
  6.5 4.7 %copy-start.1 = (f32[128]{0:T(128)S(1)}, f32[128]{0:T(128)}, u32[]{:S(2)}) copy-start(f32[128]{0:T(128)} %param.11) | copy-start | bytes 1540
  6.5 28.7 %copy-start = (f32[16,1024]{1,0:T(8,128)S(1)}, f32[16,1024]{1,0:T(8,128)}, u32[]{:S(2)}) copy-start(f32[16,1024]{1,0:T(8,128)} %param.8) | copy-start | bytes 196612
  6.5 43.9 %all-gather.9.cloned.1.call-start = ((), (), s32[]{:S(2)}) async-start(), calls=%async_computation | async-start | bytes 2621440 | tf_op jit(solution)/shard_map/all_gather | solution.py:54
Sparse Core Ops, SparseCore 0:
  9.9 38.0 all-gather.8
where the time goes:
time: 97 us; the launch traced here: 96.7 us
  blocking collectives  72.7 us (75%)
  between operations  14.1 us (15%)
  other arithmetic  4.81 us (5%)
  matrix products  3.9 us (4%)
    all_gather x4, blocking collectives, merged(): gathered = jax.tree.map(lambda a: lax.all_gather(a, axis), part)  33.8 us
    all_gather x1, blocking collectives, body(): rows = lax.all_gather(src_unit, 'shard', axis=0, tiled=True)  14.9 us
    unnamed x1, blocking collectives  14.6 us
    all_gather x1, blocking collectives, body(): lax.all_gather(inv_tgt, 'grp', axis=0, tiled=True)  9.36 us
    dot_general x1, matrix products, products(): jnp.dot(left, right.T, precision=lax.Precision.HIGHEST, preferred_element...  3.9 us
    mul x2, other arithmetic, unit_rows(): return rows * lax.rsqrt(jnp.sum(rows * rows, axis=1, keepdims=True) + 1e-06)  2.03 us
  transfers between devices with their start and end apart: 1, of which 0 were waited for; matrix products, arithmetic and copies ran while one was open for 1% of the time, Pallas kernels for 0%

commit v1 on v0

v1 whole, which is shorter than its diff:
```python
import functools
import math

import jax
import jax.numpy as jnp
from jax import lax
from jax.experimental import pallas as pl
from jax.experimental.pallas import tpu as pltpu
from jax.sharding import PartitionSpec as P

MESH = pl.DeviceIdType.MESH


def split(rows):
    unit = rows * lax.rsqrt(jnp.sum(rows * rows, axis=1, keepdims=True) + 1e-06)
    high = unit.astype(jnp.bfloat16)
    return high, (unit - high.astype(jnp.float32)).astype(jnp.bfloat16)


def kernel(
    G, S, src, inv_src, tgt, inv_tgt, out,
    X, T, TT, XX, CB, C, IS, BV, BM, L, LM, ISM,
    local_sem, z_s, z_r, f_s, f_r, r_s, r_r, sib_s, sib_r, is_s, is_r,
    cos_s, cos_r, b_s, b_r, l_s, l_r,
):
    Z = S // 2
    n, width = src.shape[0], tgt.shape[0]
    height = n * S
    HF, HR = G // 2, (G - 1) // 2
    g, s = lax.axis_index("grp"), lax.axis_index("shard")
    c, z = lax.rem(s, 2), s // 2
    sgn = 1 - 2 * c
    odd = lax.rem(g, 2)
    p = (1 - odd) * (g // 2) + odd * (G - 1 - g // 2)

    def at(r):
        q = lax.rem(p + sgn * r + G, G)
        h = q // (G // 2)
        return (1 - h) * 2 * q + h * (2 * (G - 1 - q) + 1)

    ahead = [at(r) for r in range(G)]
    zs = [z] + [jnp.bitwise_xor(z, k) for k in range(1, Z)]
    sib = s + 1 - 2 * c

    def rows(group, k, core):
        return pl.ds(pl.multiple_of((group * S + zs[k] * 2 + core) * n, n), n)

    def send(a, b, ss, rs, dev):
        cp = pltpu.make_async_remote_copy(a, b, ss, rs, device_id=dev, device_id_type=MESH)
        cp.start()
        sends.append(cp)

    def arrived(b, rs):
        pltpu.make_async_copy(b, b, rs).wait()

    sends = []
    tcopy = pltpu.make_async_copy(tgt, T, local_sem.at[0])
    tcopy.start()
    own = X.at[rows(g, 0, c)]
    scopy = pltpu.make_async_copy(src, own, local_sem.at[1])
    scopy.start()

    barrier = pltpu.get_barrier_semaphore()
    for d in range(1, S):
        pl.semaphore_signal(barrier, inc=1, device_id=(g, lax.rem(s + d, S)), device_id_type=MESH)
    for r in range(1, G):
        pl.semaphore_signal(barrier, inc=1, device_id=(ahead[r], s), device_id_type=MESH)
    pl.semaphore_wait(barrier, S + G - 2)

    for k in range(1, Z):
        send(src, own, z_s.at[k], z_r.at[k], (g, zs[k] * 2 + c))

    fwd, back = (ahead[1], s), (ahead[G - 1], s)

    def onward(piece, where, k, hop, stream):
        if stream != "r" and hop < HF:
            send(piece, where, f_s.at[hop, k], f_r.at[hop, k], fwd)
        if stream != "f" and hop < HR:
            send(piece, where, r_s.at[hop, k], r_r.at[hop, k], back)
        i = hop if stream != "r" else HF + hop
        send(piece, where, sib_s.at[i, k], sib_r.at[i, k], (g, sib))

    def prepare(group, k, i_sib):
        arrived(X.at[rows(group, k, 1 - c)], sib_r.at[i_sib, k])
        at_row = pl.multiple_of((group * S + zs[k] * 2) * n, 2 * n)
        to_row = pl.multiple_of(zs[k] * 2 * n, 2 * n)
        high, low = split(X[pl.ds(at_row, 2 * n), :])
        XX[pl.ds(to_row, 2 * n), :] = high
        XX[pl.ds(height + to_row, 2 * n), :] = low

    def block():
        w = lax.dot_general(
            XX[...], TT[...], (((1,), (1,)), ((), ())), preferred_element_type=jnp.float32
        )
        return (w[:height, :width] + (w[:height, width:] + w[height:, :width]))

    state = [None]

    def column(cos):
        logits = cos * inv_tgt[...]
        top = jnp.max(logits, axis=0, keepdims=True)
        if state[0] is not None:
            top = jnp.maximum(top, state[0][0])
        total = jnp.sum(jnp.exp(logits - top), axis=0, keepdims=True)
        if state[0] is not None:
            total = total + state[0][1] * jnp.exp(state[0][0] - top)
        state[0] = (top, total)

    def finish(r):
        cos = block()
        if r == 0:
            C[g] = cos
        else:
            CB[r - 1] = cos
            send(CB.at[r - 1], C.at[g], cos_s.at[r - 1], cos_r.at[r - 1], (ahead[r], s))
        column(cos)

    for t in range(Z + HF):
        for h in range(HF, -1, -1):
            k = t - h
            if not 0 <= k < Z:
                continue
            if h == 0:
                if k == 0:
                    onward(src, own, 0, 0, "own")
                else:
                    where = X.at[rows(g, k, c)]
                    arrived(where, z_r.at[k])
                    onward(where, where, k, 0, "own")
                continue
            where = X.at[rows(ahead[G - h], k, c)]
            arrived(where, f_r.at[h - 1, k])
            onward(where, where, k, h, "f")
            if h <= HR:
                where = X.at[rows(ahead[h], k, c)]
                arrived(where, r_r.at[h - 1, k])
                onward(where, where, k, h, "r")
        if t == 0:
            lane = lax.broadcasted_iota(jnp.int32, (n, n), 1)
            sub = lax.broadcasted_iota(jnp.int32, (n, n), 0)
            column_inv = jnp.sum(
                jnp.where(lane == sub, jnp.broadcast_to(inv_src[...], (n, n)), 0.0),
                axis=1, keepdims=True,
            )
            ISM[...] = jnp.broadcast_to(column_inv, (n, 128))
            mine = pl.ds(pl.multiple_of(s * n, n), n)
            IS[mine, :] = ISM[...]
            for d in range(1, S):
                send(ISM, IS.at[mine, :], is_s.at[d], is_r.at[d], (g, lax.rem(s + d, S)))
            tcopy.wait()
            for i in range(0, width, 32):
                high, low = split(T[i : i + 32, :])
                TT[i : i + 32, :] = high
                TT[width + i : width + i + 32, :] = low
            scopy.wait()
        if 1 <= t <= Z:
            prepare(g, t - 1, 0)
        if t == Z:
            finish(0)

    for h in range(1, HF + 1):
        if h <= HR:
            for k in range(Z):
                prepare(ahead[G - h], k, HF + h)
            finish(G - h)
        for k in range(Z):
            prepare(ahead[h], k, h)
        finish(h)

    top, total = state[0]
    b = top + jnp.log(total) - math.log(height * G)
    BM[0:1, :] = b
    BM[1:2, :] = inv_tgt[...]
    BV[g] = BM[...]
    for r in range(1, G):
        send(BM, BV.at[g], b_s.at[r], b_r.at[r], (ahead[r], s))

    for d in range(1, S):
        frm = lax.rem(s + S - d, S)
        arrived(IS.at[pl.ds(pl.multiple_of(frm * n, n), n), :], is_r.at[d])
    for r in range(1, G):
        arrived(C.at[ahead[G - r]], cos_r.at[r - 1])

    inv_rows = IS[...]
    logits = [C[j] * inv_rows for j in range(G)]
    top = functools.reduce(jnp.maximum, logits)
    top = jnp.max(top, axis=1, keepdims=True)
    total = jnp.sum(sum(jnp.exp(x - top) for x in logits), axis=1, keepdims=True)
    part = top + jnp.log(total)
    LM[...] = jnp.transpose(jnp.broadcast_to(part, (height, 128)))[:8, :]
    L[s] = LM[...]
    for d in range(1, S):
        send(LM, L.at[s], l_s.at[d], l_r.at[d], (g, lax.rem(s + d, S)))
    for r in range(1, G):
        arrived(BV.at[ahead[G - r]], b_r.at[r])
    for d in range(1, S):
        arrived(L.at[lax.rem(s + S - d, S)], l_r.at[d])

    parts = L[...]
    top = jnp.max(parts, axis=0)
    a = top + jnp.log(jnp.sum(jnp.exp(parts - top[None]), axis=0)) - math.log(G * width * S)
    a = jnp.transpose(jnp.broadcast_to(a[:1, :], (128, height)))
    for j in range(G):
        b = BV[j, 0:1, :]
        scale = 0.5 * (inv_rows + BV[j, 1:2, :])
        both = jnp.maximum(a, b) + jnp.log(1.0 + jnp.exp(-jnp.abs(a - b)))
        out[:, j * width : (j + 1) * width] = C[j] * scale - (both - math.log(2.0))

    for cp in sends:
        cp.wait_send()


def body(src, inv_src, tgt, inv_tgt):
    G, S = lax.axis_size("grp"), lax.axis_size("shard")
    n, depth = src.shape
    width = tgt.shape[0]
    height = n * S
    Z, HF, HR = S // 2, G // 2, (G - 1) // 2
    f32, bf16 = jnp.float32, jnp.bfloat16
    dma = pltpu.SemaphoreType.DMA
    vmem = pl.BlockSpec(memory_space=pltpu.VMEM)
    anyw = pl.BlockSpec(memory_space=pl.ANY)
    return pl.pallas_call(
        functools.partial(kernel, G, S),
        out_shape=jax.ShapeDtypeStruct((height, G * width), f32),
        in_specs=[anyw, vmem, anyw, vmem],
        out_specs=vmem,
        scratch_shapes=[
            pltpu.VMEM((G * height, depth), f32),
            pltpu.VMEM((width, depth), f32),
            pltpu.VMEM((2 * width, depth), bf16),
            pltpu.VMEM((2 * height, depth), bf16),
            pltpu.VMEM((G - 1, height, width), f32),
            pltpu.VMEM((G, height, width), f32),
            pltpu.VMEM((height, 128), f32),
            pltpu.VMEM((G, 8, width), f32),
            pltpu.VMEM((8, width), f32),
            pltpu.VMEM((S, 8, height), f32),
            pltpu.VMEM((8, height), f32),
            pltpu.VMEM((n, 128), f32),
            dma((2,)),
            dma((Z,)), dma((Z,)),
            dma((HF, Z)), dma((HF, Z)),
            dma((HR, Z)), dma((HR, Z)),
            dma((HF + HR + 1, Z)), dma((HF + HR + 1, Z)),
            dma((S,)), dma((S,)),
            dma((G - 1,)), dma((G - 1,)),
            dma((G,)), dma((G,)),
            dma((S,)), dma((S,)),
        ],
        compiler_params=pltpu.CompilerParams(
            collective_id=0, has_side_effects=True, vmem_limit_bytes=56 * 2**20
        ),
        cost_estimate=pl.CostEstimate(
            flops=8 * G * height * width * depth, bytes_accessed=8 * width * depth,
            transcendentals=4 * G * height * width,
        ),
    )(src, inv_src.reshape(1, n), tgt, inv_tgt.reshape(1, width))


def solution(mesh):
    return jax.shard_map(
        body,
        mesh=mesh,
        in_specs=(
            P(("grp", "shard"), None),
            P(("grp", "shard")),
            P(("shard", "grp"), None),
            P(("shard", "grp")),
        ),
        out_specs=P("grp", "shard"),
        check_vma=False,
    )
```

time: 97 us -> 40.4 us (0.42)
  blocking collectives: 72.7 us -> 0 us
  Pallas kernels: 0 us -> 38.5 us
  between operations: 14.1 us -> 0.01 us
  other arithmetic: 4.81 us -> 0 us
  matrix products: 3.9 us -> 0 us
    all_gather x6 -> x0, blocking collectives: 58.1 us -> none  [the longest x4 33.8 us: merged(): gathered = jax.tree.map(lambda a: lax.all_gather(a, axis), part)]
    pallas_call x0 -> x1, Pallas kernels: none -> 38.5 us  [body(): pl.pallas_call(functools.partial(kernel, G, S), out_shape=jax.ShapeDtypeS...]
    unnamed x1 -> x0, blocking collectives: 14.6 us -> none
    dot_general x1 -> x0, matrix products: 3.9 us -> none  [products(): jnp.dot(left, right.T, precision=lax.Precision.HIGHEST, preferred_element...]
    mul x2 -> x0, other arithmetic: 2.03 us -> none  [unit_rows(): return rows * lax.rsqrt(jnp.sum(rows * rows, axis=1, keepdims=True) + 1e-06)]
    reduce_sum x3 -> x0, other arithmetic: 1.51 us -> none  [the longest x2 1.31 us: unit_rows(): return rows * lax.rsqrt(jnp.sum(rows * rows, axis=1, keepdims=True) + 1e-06)]
    sub x3 -> x0, other arithmetic: 0.99 us -> none  [the longest x1 0.98 us: body(): sims_all * scale]
  transfers between devices with their start and end apart: 1 -> 0, of which waited for: 0 -> 0; matrix products, arithmetic and copies ran while one was open for 1% -> 0% of each run, Pallas kernels for 0% -> 0%
where the time goes in v1:
time: 40.4 us; the launch traced here: 40.2 us
  Pallas kernels  38.5 us (95%)
  local copies, waits for them, and re-layouts  1.67 us (4%)
    pallas_call x1, Pallas kernels, body(): pl.pallas_call(functools.partial(kernel, G, S), out_shape=jax.ShapeDtypeS...  38.5 us
    unnamed x1, local copies, waits for them, and re-layouts  1.67 us

profile of v1, /device:TPU:0, one launch (start us, length us, event | category | flops | bytes accessed | tf_op | source)
XLA Modules:
  0.0 40.2 jit_solution(9956487986494027656)
XLA Ops:
  0.0 38.5 %shard_map.46 = f32[128,512]{1,0:T(8,128)} custom-call(f32[16,1024]{1,0:T(8,128)} %src.1, f32[1,16]{1,0:T(1,128)} %bitcast.2, f32[128,1024]{1,0:T(8,128)} %tgt.1, f32[1,128]{1,0:T(1,128)} %bitcast.3), custom_call_target="tpu_custom_call" | custom-call | flops 536870912 | bytes 1048576 | tf_op jit(solution)/shard_map/pallas_call | solution.py:223
  38.5 1.7 %copy.6 = f32[128,512]{1,0:T(8,128)} copy(f32[128,512]{1,0:T(8,128)} %shard_map.46) | data formatting | bytes 524288

commit v2 on v1

v2 whole, which is shorter than its diff:
```python
import functools
import math

import jax
import jax.numpy as jnp
from jax import lax
from jax.experimental import pallas as pl
from jax.experimental.pallas import tpu as pltpu
from jax.sharding import PartitionSpec as P

MESH = pl.DeviceIdType.MESH


def split(rows):
    unit = rows * lax.rsqrt(jnp.sum(rows * rows, axis=1, keepdims=True) + 1e-06)
    high = unit.astype(jnp.bfloat16)
    return high, (unit - high.astype(jnp.float32)).astype(jnp.bfloat16)


def kernel(
    G, S, src, inv_src, tgt, inv_tgt, out,
    X, T, TT, XX, TI, CB, C, IS, ISM, BM, BV, LM, L,
    local_sem, t_s, t_r, z_s, z_r, f_s, f_r, r_s, r_r, is_s, is_r,
    cos_s, cos_r, b_s, b_r, l_s, l_r,
):
    Z = S // 2
    n, width = src.shape[0], tgt.shape[0]
    half = n * Z
    height = n * S
    HF, HR = G // 2, (G - 1) // 2
    g, s = lax.axis_index("grp"), lax.axis_index("shard")
    c, z = lax.rem(s, 2), s // 2
    sgn = 1 - 2 * c
    odd = lax.rem(g, 2)
    p = (1 - odd) * (g // 2) + odd * (G - 1 - g // 2)

    def at(r):
        q = lax.rem(p + sgn * r + G, G)
        h = q // (G // 2)
        return (1 - h) * 2 * q + h * (2 * (G - 1 - q) + 1)

    ahead = [at(r) for r in range(G)]
    zs = [z] + [jnp.bitwise_xor(z, k) for k in range(1, Z)]
    other = 1 - c
    sib = z * 2 + other

    def rows(k):
        return pl.ds(pl.multiple_of(zs[k] * n, n), n)

    def send(a, b, ss, rs, dev):
        cp = pltpu.make_async_remote_copy(a, b, ss, rs, device_id=dev, device_id_type=MESH)
        cp.start()
        sends.append(cp)

    def arrived(b, rs):
        pltpu.make_async_copy(b, b, rs).wait()

    def signal(dev):
        pl.semaphore_signal(barrier, inc=1, device_id=dev, device_id_type=MESH)

    sends = []
    barrier = pltpu.get_barrier_semaphore()
    for d in range(1, S):
        signal((g, lax.rem(s + d, S)))
    for r in range(1, G):
        for o in range(2):
            signal((ahead[r], z * 2 + o))
    mine_t = pl.ds(pl.multiple_of(c * width, width), width)
    their_t = pl.ds(pl.multiple_of(other * width, width), width)
    tcopy = pltpu.make_async_copy(tgt, T.at[mine_t, :], local_sem.at[0])
    tcopy.start()
    scopy = pltpu.make_async_copy(src, X.at[g, rows(0), :], local_sem.at[1])
    scopy.start()
    TI[c] = jnp.broadcast_to(inv_tgt[...], (8, width))
    pl.semaphore_wait(barrier, S - 1 + 2 * (G - 1))

    for k in range(1, Z):
        send(src, X.at[g, rows(0), :], z_s.at[k], z_r.at[k], (g, zs[k] * 2 + c))

    fwd, back = (ahead[1], s), (ahead[G - 1], s)

    def onward(piece, where, k, hop, stream):
        if stream != "r" and hop < HF:
            send(piece, where, f_s.at[hop, k], f_r.at[hop, k], fwd)
        if stream != "f" and hop < HR:
            send(piece, where, r_s.at[hop, k], r_r.at[hop, k], back)

    def prepare(r, k):
        high, low = split(X[ahead[r], rows(k), :])
        XX[r, rows(k), :] = high
        XX[r, pl.ds(pl.multiple_of(half + zs[k] * n, n), n), :] = low

    state = [None, None]

    def column(o, cos):
        logits = cos * TI[o, 0:1, :]
        top = jnp.max(logits, axis=0, keepdims=True)
        if state[o] is not None:
            top = jnp.maximum(top, state[o][0])
        total = jnp.sum(jnp.exp(logits - top), axis=0, keepdims=True)
        if state[o] is not None:
            total = total + state[o][1] * jnp.exp(state[o][0] - top)
        state[o] = (top, total)

    def finish(r):
        w = lax.dot_general(
            XX[r], TT[...], (((1,), (1,)), ((), ())), preferred_element_type=jnp.float32
        )
        cos = w[:half, : 2 * width] + (w[:half, 2 * width :] + w[half:, : 2 * width])
        parts = [cos[:, o * width : (o + 1) * width] for o in range(2)]
        for o in range(2):
            CB[r, o] = parts[o]
            if r > 0:
                send(CB.at[r, o], C.at[g, c], cos_s.at[r, o], cos_r.at[r, c], (ahead[r], z * 2 + o))
        if r == 0:
            C[g, c] = CB[0, c]
            send(CB.at[0, other], C.at[g, c], cos_s.at[0, 0], cos_r.at[0, c], (g, sib))
        for o in range(2):
            column(o, parts[o])

    def targets(o):
        for i in range(0, width, 32):
            high, low = split(T[pl.ds(pl.multiple_of(o * width + i, 32), 32), :])
            TT[pl.ds(pl.multiple_of(o * width + i, 32), 32), :] = high
            TT[pl.ds(pl.multiple_of((2 + o) * width + i, 32), 32), :] = low

    for t in range(Z + HF):
        ready = []
        for h in range(HF, -1, -1):
            k = t - h
            if not 0 <= k < Z:
                continue
            if h == 0:
                where = X.at[g, rows(k), :]
                if k == 0:
                    onward(src, where, 0, 0, "own")
                else:
                    arrived(where, z_r.at[k])
                    onward(where, where, k, 0, "own")
                    ready.append((0, k))
                continue
            where = X.at[ahead[G - h], rows(k), :]
            arrived(where, f_r.at[h - 1, k])
            onward(where, where, k, h, "f")
            ready.append((G - h, k))
            if h <= HR:
                where = X.at[ahead[h], rows(k), :]
                arrived(where, r_r.at[h - 1, k])
                onward(where, where, k, h, "r")
                ready.append((h, k))
        if t == 0:
            send(tgt, T.at[mine_t, :], t_s.at[0], t_r.at[0], (g, sib))
            send(TI.at[c], TI.at[c], t_s.at[1], t_r.at[1], (g, sib))
            lane = lax.broadcasted_iota(jnp.int32, (n, n), 1)
            sub = lax.broadcasted_iota(jnp.int32, (n, n), 0)
            column_inv = jnp.sum(
                jnp.where(lane == sub, jnp.broadcast_to(inv_src[...], (n, n)), 0.0),
                axis=1, keepdims=True,
            )
            ISM[...] = jnp.broadcast_to(column_inv, (n, 128))
            IS[c, rows(0), :] = ISM[...]
            for d in range(1, S):
                send(ISM, IS.at[c, rows(0), :], is_s.at[d], is_r.at[d], (g, lax.rem(s + d, S)))
            scopy.wait()
            prepare(0, 0)
            tcopy.wait()
            targets(c)
        if t == 1:
            arrived(T.at[their_t, :], t_r.at[0])
            arrived(TI.at[other], t_r.at[1])
            targets(other)
        for r, k in ready:
            prepare(r, k)
            if k == Z - 1:
                finish(r)

    for o in range(2):
        top, total = state[o]
        BM[o] = TI[o]
        BM[o, 0:1, :] = top + jnp.log(total)
    BV[g, c] = BM[c]
    send(BM.at[other], BV.at[g, c], b_s.at[0, 0], b_r.at[0, c], (g, sib))
    for r in range(1, G):
        for o in range(2):
            send(BM.at[o], BV.at[g, c], b_s.at[r, o], b_r.at[r, c], (ahead[r], z * 2 + o))

    for d in range(1, S):
        frm = lax.rem(s + S - d, S)
        place = pl.ds(pl.multiple_of(frm // 2 * n, n), n)
        arrived(IS.at[lax.rem(frm, 2), place, :], is_r.at[d])

    froms = [(g, other, 0)]
    for r in range(1, G):
        froms += [(ahead[G - r], c, r), (ahead[r], other, r)]
    for group, core, r in froms:
        arrived(C.at[group, core], cos_r.at[r, core])

    inv_rows = IS[...]
    logits = [C[j] * inv_rows for j in range(G)]
    top = jnp.max(functools.reduce(jnp.maximum, logits), axis=2, keepdims=True)
    total = jnp.sum(sum(jnp.exp(x - top) for x in logits), axis=2, keepdims=True)
    part = (top + jnp.log(total)).reshape(height, 1)
    LM[...] = jnp.transpose(jnp.broadcast_to(part, (height, 128)))[:8, :]
    L[s] = LM[...]
    for d in range(1, S):
        send(LM, L.at[s], l_s.at[d], l_r.at[d], (g, lax.rem(s + d, S)))
    for group, core, r in froms:
        arrived(BV.at[group, core], b_r.at[r, core])
    for d in range(1, S):
        arrived(L.at[lax.rem(s + S - d, S)], l_r.at[d])

    parts = L[...]
    top = jnp.max(parts, axis=0)
    a = top + jnp.log(jnp.sum(jnp.exp(parts - top[None]), axis=0)) - math.log(G * width * S)
    a = jnp.transpose(jnp.broadcast_to(a[:1, :], (128, height))).reshape(2, half, 128)
    for j in range(G):
        first, second = BV[j, 0, 0:1, :], BV[j, 1, 0:1, :]
        b = jnp.maximum(first, second) + jnp.log(1.0 + jnp.exp(-jnp.abs(first - second)))
        b = b - math.log(height * G)
        both = jnp.maximum(a, b) + jnp.log(1.0 + jnp.exp(-jnp.abs(a - b)))
        scale = 0.5 * (inv_rows + BV[j, 0, 1:2, :])
        margin = C[j] * scale - (both - math.log(2.0))
        for o in range(2):
            for q in range(Z):
                place = (q * 2 + o) * n
                out[place : place + n, j * width : (j + 1) * width] = margin[o, q * n : (q + 1) * n]

    for cp in sends:
        cp.wait_send()


def body(src, inv_src, tgt, inv_tgt):
    G, S = lax.axis_size("grp"), lax.axis_size("shard")
    n, depth = src.shape
    width = tgt.shape[0]
    height = n * S
    half = height // 2
    Z, HF, HR = S // 2, G // 2, (G - 1) // 2
    f32, bf16 = jnp.float32, jnp.bfloat16
    dma = pltpu.SemaphoreType.DMA
    vmem = pl.BlockSpec(memory_space=pltpu.VMEM)
    anyw = pl.BlockSpec(memory_space=pl.ANY)
    return pl.pallas_call(
        functools.partial(kernel, G, S),
        out_shape=jax.ShapeDtypeStruct((height, G * width), f32),
        in_specs=[anyw, vmem, anyw, vmem],
        out_specs=vmem,
        scratch_shapes=[
            pltpu.VMEM((G, half, depth), f32),
            pltpu.VMEM((2 * width, depth), f32),
            pltpu.VMEM((4 * width, depth), bf16),
            pltpu.VMEM((G, 2 * half, depth), bf16),
            pltpu.VMEM((2, 8, width), f32),
            pltpu.VMEM((G, 2, half, width), f32),
            pltpu.VMEM((G, 2, half, width), f32),
            pltpu.VMEM((2, half, 128), f32),
            pltpu.VMEM((n, 128), f32),
            pltpu.VMEM((2, 8, width), f32),
            pltpu.VMEM((G, 2, 8, width), f32),
            pltpu.VMEM((8, height), f32),
            pltpu.VMEM((S, 8, height), f32),
            dma((2,)),
            dma((2,)), dma((2,)),
            dma((Z,)), dma((Z,)),
            dma((HF, Z)), dma((HF, Z)),
            dma((HR, Z)), dma((HR, Z)),
            dma((S,)), dma((S,)),
            dma((G, 2)), dma((G, 2)),
            dma((G, 2)), dma((G, 2)),
            dma((S,)), dma((S,)),
        ],
        compiler_params=pltpu.CompilerParams(
            collective_id=0, has_side_effects=True, vmem_limit_bytes=56 * 2**20
        ),
        cost_estimate=pl.CostEstimate(
            flops=8 * G * height * width * depth, bytes_accessed=8 * width * depth,
            transcendentals=4 * G * height * width,
        ),
    )(src, inv_src.reshape(1, n), tgt, inv_tgt.reshape(1, width))


def solution(mesh):
    return jax.shard_map(
        body,
        mesh=mesh,
        in_specs=(
            P(("grp", "shard"), None),
            P(("grp", "shard")),
            P(("shard", "grp"), None),
            P(("shard", "grp")),
        ),
        out_specs=P("grp", "shard"),
        check_vma=False,
    )
```

time: 40.4 us -> 38.4 us (0.950)
  Pallas kernels: 38.5 us -> 36.6 us
    pallas_call x1, Pallas kernels: 38.5 us -> 36.6 us  [body(): pl.pallas_call(functools.partial(kernel, G, S), out_shape=jax.ShapeDtypeS...]
where the time goes in v2:
time: 38.4 us; the launch traced here: 38.2 us
  Pallas kernels  36.6 us (95%)
  local copies, waits for them, and re-layouts  1.67 us (4%)
    pallas_call x1, Pallas kernels, body(): pl.pallas_call(functools.partial(kernel, G, S), out_shape=jax.ShapeDtypeS...  36.6 us
    unnamed x1, local copies, waits for them, and re-layouts  1.67 us

profile of v2, /device:TPU:0, one launch (start us, length us, event | category | flops | bytes accessed | tf_op | source)
XLA Modules:
  0.0 38.2 jit_solution(2401172822218069274)
XLA Ops:
  0.0 36.6 %shard_map.46 = f32[128,512]{1,0:T(8,128)} custom-call(f32[16,1024]{1,0:T(8,128)} %src.1, f32[1,16]{1,0:T(1,128)} %bitcast.2, f32[128,1024]{1,0:T(8,128)} %tgt.1, f32[1,128]{1,0:T(1,128)} %bitcast.3), custom_call_target="tpu_custom_call" | custom-call | flops 536870912 | bytes 1048576 | tf_op jit(solution)/shard_map/pallas_call | solution.py:243
  36.6 1.7 %copy.6 = f32[128,512]{1,0:T(8,128)} copy(f32[128,512]{1,0:T(8,128)} %shard_map.46) | data formatting | bytes 524288

commit v3 on v2

--- a/solution.py
+++ b/solution.py
@@ -40,6 +40,9 @@
         return (1 - h) * 2 * q + h * (2 * (G - 1 - q) + 1)
 
     ahead = [at(r) for r in range(G)]
+    order = [0]
+    for r in range(1, HF + 1):
+        order += [G - r] if G - r == r else [G - r, r]
     zs = [z] + [jnp.bitwise_xor(z, k) for k in range(1, Z)]
     other = 1 - c
     sib = z * 2 + other
@@ -66,7 +69,6 @@
         for o in range(2):
             signal((ahead[r], z * 2 + o))
     mine_t = pl.ds(pl.multiple_of(c * width, width), width)
-    their_t = pl.ds(pl.multiple_of(other * width, width), width)
     tcopy = pltpu.make_async_copy(tgt, T.at[mine_t, :], local_sem.at[0])
     tcopy.start()
     scopy = pltpu.make_async_copy(src, X.at[g, rows(0), :], local_sem.at[1])
@@ -87,8 +89,9 @@
 
     def prepare(r, k):
         high, low = split(X[ahead[r], rows(k), :])
-        XX[r, rows(k), :] = high
-        XX[r, pl.ds(pl.multiple_of(half + zs[k] * n, n), n), :] = low
+        i = order.index(r)
+        XX[i, rows(k), :] = high
+        XX[i, pl.ds(pl.multiple_of(half + zs[k] * n, n), n), :] = low
 
     state = [None, None]
 
@@ -102,28 +105,43 @@
             total = total + state[o][1] * jnp.exp(state[o][0] - top)
         state[o] = (top, total)
 
-    def finish(r):
+    def finish(first, last):
+        count = last - first
         w = lax.dot_general(
-            XX[r], TT[...], (((1,), (1,)), ((), ())), preferred_element_type=jnp.float32
-        )
-        cos = w[:half, : 2 * width] + (w[:half, 2 * width :] + w[half:, : 2 * width])
-        parts = [cos[:, o * width : (o + 1) * width] for o in range(2)]
-        for o in range(2):
-            CB[r, o] = parts[o]
-            if r > 0:
-                send(CB.at[r, o], C.at[g, c], cos_s.at[r, o], cos_r.at[r, c], (ahead[r], z * 2 + o))
-        if r == 0:
-            C[g, c] = CB[0, c]
-            send(CB.at[0, other], C.at[g, c], cos_s.at[0, 0], cos_r.at[0, c], (g, sib))
-        for o in range(2):
-            column(o, parts[o])
-
-    def targets(o):
-        for i in range(0, width, 32):
-            high, low = split(T[pl.ds(pl.multiple_of(o * width + i, 32), 32), :])
-            TT[pl.ds(pl.multiple_of(o * width + i, 32), 32), :] = high
-            TT[pl.ds(pl.multiple_of((2 + o) * width + i, 32), 32), :] = low
-
+            XX[first:last].reshape(count * 2 * half, XX.shape[2]), TT[...],
+            (((1,), (1,)), ((), ())), preferred_element_type=jnp.float32,
+        ).reshape(count, 2 * half, 4 * width)
+        blocks = []
+        for i in range(count):
+            r, v = order[first + i], w[i]
+            cos = v[:half, : 2 * width] + (v[:half, 2 * width :] + v[half:, : 2 * width])
+            parts = [cos[:, o * width : (o + 1) * width] for o in range(2)]
+            blocks.append(parts)
+            for o in range(2):
+                CB[r, o] = parts[o]
+                if r > 0:
+                    send(
+                        CB.at[r, o], C.at[g, c], cos_s.at[r, o], cos_r.at[r, c],
+                        (ahead[r], z * 2 + o),
+                    )
+            if r == 0:
+                C[g, c] = CB[0, c]
+                send(CB.at[0, other], C.at[g, c], cos_s.at[0, 0], cos_r.at[0, c], (g, sib))
+        for parts in blocks:
+            for o in range(2):
+                column(o, parts[o])
+
+    chunk = width // 4
+
+    def piece_of(o, i):
+        return pl.ds(pl.multiple_of(o * width + i * chunk, chunk), chunk)
+
+    def targets(o, i):
+        high, low = split(T[piece_of(o, i), :])
+        TT[piece_of(o, i), :] = high
+        TT[piece_of(o + 2, i), :] = low
+
+    finished = 0
     for t in range(Z + HF):
         ready = []
         for h in range(HF, -1, -1):
@@ -148,9 +166,13 @@
                 arrived(where, r_r.at[h - 1, k])
                 onward(where, where, k, h, "r")
                 ready.append((h, k))
+        if t < 4:
+            send(
+                tgt.at[pl.ds(t * chunk, chunk), :], T.at[piece_of(c, t), :],
+                t_s.at[t], t_r.at[t], (g, sib),
+            )
         if t == 0:
-            send(tgt, T.at[mine_t, :], t_s.at[0], t_r.at[0], (g, sib))
-            send(TI.at[c], TI.at[c], t_s.at[1], t_r.at[1], (g, sib))
+            send(TI.at[c], TI.at[c], t_s.at[4], t_r.at[4], (g, sib))
             lane = lax.broadcasted_iota(jnp.int32, (n, n), 1)
             sub = lax.broadcasted_iota(jnp.int32, (n, n), 0)
             column_inv = jnp.sum(
@@ -164,15 +186,19 @@
             scopy.wait()
             prepare(0, 0)
             tcopy.wait()
-            targets(c)
-        if t == 1:
-            arrived(T.at[their_t, :], t_r.at[0])
-            arrived(TI.at[other], t_r.at[1])
-            targets(other)
+            for i in range(4):
+                targets(c, i)
         for r, k in ready:
             prepare(r, k)
-            if k == Z - 1:
-                finish(r)
+        if 1 <= t <= 4:
+            arrived(T.at[piece_of(other, t - 1), :], t_r.at[t - 1])
+            targets(other, t - 1)
+        if t == 4:
+            arrived(TI.at[other], t_r.at[4])
+        if t >= Z:
+            done = len([r for r, k in ready if k == Z - 1])
+            finish(finished, finished + done + (t == Z))
+            finished += done + (t == Z)
 
     for o in range(2):
         top, total = state[o]
@@ -260,7 +286,7 @@
             pltpu.VMEM((8, height), f32),
             pltpu.VMEM((S, 8, height), f32),
             dma((2,)),
-            dma((2,)), dma((2,)),
+            dma((5,)), dma((5,)),
             dma((Z,)), dma((Z,)),
             dma((HF, Z)), dma((HF, Z)),
             dma((HR, Z)), dma((HR, Z)),

time: 38.4 us -> 37.7 us (0.982)
  Pallas kernels: 36.6 us -> 35.9 us
    pallas_call x1, Pallas kernels: 36.6 us -> 35.9 us  [body(): pl.pallas_call(functools.partial(kernel, G, S), out_shape=jax.ShapeDtypeS...]
where the time goes in v3:
time: 37.7 us; the launch traced here: 37.6 us
  Pallas kernels  35.9 us (95%)
  local copies, waits for them, and re-layouts  1.67 us (4%)
    pallas_call x1, Pallas kernels, body(): pl.pallas_call(functools.partial(kernel, G, S), out_shape=jax.ShapeDtypeS...  35.9 us
    unnamed x1, local copies, waits for them, and re-layouts  1.67 us

profile of v3, /device:TPU:0, one launch (start us, length us, event | category | flops | bytes accessed | tf_op | source)
XLA Modules:
  0.0 37.6 jit_solution(3886827758523454007)
XLA Ops:
  0.0 35.9 %shard_map.46 = f32[128,512]{1,0:T(8,128)} custom-call(f32[16,1024]{1,0:T(8,128)} %src.1, f32[1,16]{1,0:T(1,128)} %bitcast.2, f32[128,1024]{1,0:T(8,128)} %tgt.1, f32[1,128]{1,0:T(1,128)} %bitcast.3), custom_call_target="tpu_custom_call" | custom-call | flops 536870912 | bytes 1048576 | tf_op jit(solution)/shard_map/pallas_call | solution.py:269
  35.9 1.7 %copy.6 = f32[128,512]{1,0:T(8,128)} copy(f32[128,512]{1,0:T(8,128)} %shard_map.46) | data formatting | bytes 524288

commit v4 on v3

--- a/solution.py
+++ b/solution.py
@@ -19,8 +19,8 @@
 
 def kernel(
     G, S, src, inv_src, tgt, inv_tgt, out,
-    X, T, TT, XX, TI, CB, C, IS, ISM, BM, BV, LM, L,
-    local_sem, t_s, t_r, z_s, z_r, f_s, f_r, r_s, r_r, is_s, is_r,
+    X, T, TT, XX, TI, CB, C, IS, ISM, IM, IG, BM, BV, LM, L,
+    local_sem, t_s, t_r, z_s, z_r, f_s, f_r, r_s, r_r, is_s, is_r, ig_s, ig_r,
     cos_s, cos_r, b_s, b_r, l_s, l_r,
 ):
     Z = S // 2
@@ -63,18 +63,17 @@
 
     sends = []
     barrier = pltpu.get_barrier_semaphore()
-    for d in range(1, S):
-        signal((g, lax.rem(s + d, S)))
-    for r in range(1, G):
-        for o in range(2):
-            signal((ahead[r], z * 2 + o))
+    for r in range(G):
+        for d in range(S):
+            if (r, d) != (0, 0):
+                signal((ahead[r], lax.rem(s + d, S)))
     mine_t = pl.ds(pl.multiple_of(c * width, width), width)
     tcopy = pltpu.make_async_copy(tgt, T.at[mine_t, :], local_sem.at[0])
     tcopy.start()
     scopy = pltpu.make_async_copy(src, X.at[g, rows(0), :], local_sem.at[1])
     scopy.start()
     TI[c] = jnp.broadcast_to(inv_tgt[...], (8, width))
-    pl.semaphore_wait(barrier, S - 1 + 2 * (G - 1))
+    pl.semaphore_wait(barrier, G * S - 1)
 
     for k in range(1, Z):
         send(src, X.at[g, rows(0), :], z_s.at[k], z_r.at[k], (g, zs[k] * 2 + c))
@@ -92,6 +91,37 @@
         i = order.index(r)
         XX[i, rows(k), :] = high
         XX[i, pl.ds(pl.multiple_of(half + zs[k] * n, n), n), :] = low
+
+    wide = L.shape[3]
+
+    def lying(x):
+        x = jnp.broadcast_to(x, (half, 128))
+        return jnp.transpose(jnp.concatenate([x] * (wide // half), axis=0))[:8, :]
+
+    def standing(x):
+        return jnp.transpose(jnp.broadcast_to(x, (128, wide)))[:half, :]
+
+    def row_sums(r, parts):
+        if r == 0:
+            inv = IS[c]
+        else:
+            arrived(IG.at[ahead[r]], ig_r.at[G - r])
+            inv = standing(IG[ahead[r], 0:1, :])
+        logits = [x * inv for x in parts]
+        top = jnp.max(jnp.maximum(logits[0], logits[1]), axis=1, keepdims=True)
+        total = jnp.sum(
+            jnp.exp(logits[0] - top) + jnp.exp(logits[1] - top), axis=1, keepdims=True
+        )
+        LM[r] = lying(top + jnp.log(total))
+        where = L.at[c, z * G + g]
+        for d in range(S):
+            if (r, d) == (0, 0):
+                L[c, z * G + g] = LM[0]
+            else:
+                send(
+                    LM.at[r], where, l_s.at[r, d], l_r.at[r, d],
+                    (ahead[r], lax.rem(s + d, S)),
+                )
 
     state = [None, None]
 
@@ -127,6 +157,8 @@
             if r == 0:
                 C[g, c] = CB[0, c]
                 send(CB.at[0, other], C.at[g, c], cos_s.at[0, 0], cos_r.at[0, c], (g, sib))
+        for i, parts in enumerate(blocks):
+            row_sums(order[first + i], parts)
         for parts in blocks:
             for o in range(2):
                 column(o, parts[o])
@@ -195,6 +227,14 @@
             targets(other, t - 1)
         if t == 4:
             arrived(TI.at[other], t_r.at[4])
+        if t == 1:
+            for d in range(1, S):
+                frm = lax.rem(s + S - d, S)
+                place = pl.ds(pl.multiple_of(frm // 2 * n, n), n)
+                arrived(IS.at[lax.rem(frm, 2), place, :], is_r.at[d])
+            IM[...] = lying(IS[c])
+            for r in range(1, G):
+                send(IM, IG.at[g], ig_s.at[r], ig_r.at[r], (ahead[r], s))
         if t >= Z:
             done = len([r for r, k in ready if k == Z - 1])
             finish(finished, finished + done + (t == Z))
@@ -210,11 +250,6 @@
         for o in range(2):
             send(BM.at[o], BV.at[g, c], b_s.at[r, o], b_r.at[r, c], (ahead[r], z * 2 + o))
 
-    for d in range(1, S):
-        frm = lax.rem(s + S - d, S)
-        place = pl.ds(pl.multiple_of(frm // 2 * n, n), n)
-        arrived(IS.at[lax.rem(frm, 2), place, :], is_r.at[d])
-
     froms = [(g, other, 0)]
     for r in range(1, G):
         froms += [(ahead[G - r], c, r), (ahead[r], other, r)]
@@ -222,23 +257,22 @@
         arrived(C.at[group, core], cos_r.at[r, core])
 
     inv_rows = IS[...]
-    logits = [C[j] * inv_rows for j in range(G)]
-    top = jnp.max(functools.reduce(jnp.maximum, logits), axis=2, keepdims=True)
-    total = jnp.sum(sum(jnp.exp(x - top) for x in logits), axis=2, keepdims=True)
-    part = (top + jnp.log(total)).reshape(height, 1)
-    LM[...] = jnp.transpose(jnp.broadcast_to(part, (height, 128)))[:8, :]
-    L[s] = LM[...]
-    for d in range(1, S):
-        send(LM, L.at[s], l_s.at[d], l_r.at[d], (g, lax.rem(s + d, S)))
     for group, core, r in froms:
         arrived(BV.at[group, core], b_r.at[r, core])
-    for d in range(1, S):
-        arrived(L.at[lax.rem(s + S - d, S)], l_r.at[d])
-
-    parts = L[...]
-    top = jnp.max(parts, axis=0)
-    a = top + jnp.log(jnp.sum(jnp.exp(parts - top[None]), axis=0)) - math.log(G * width * S)
-    a = jnp.transpose(jnp.broadcast_to(a[:1, :], (128, height))).reshape(2, half, 128)
+    for d in range(S):
+        frm = lax.rem(s + S - d, S)
+        for r in range(G):
+            if (r, d) != (0, 0):
+                group = ahead[(G - r) % G] if d % 2 == 0 else ahead[r]
+                arrived(L.at[lax.rem(frm, 2), frm // 2 * G + group], l_r.at[r, d])
+
+    a = []
+    for o in range(2):
+        parts = L[o]
+        top = jnp.max(parts, axis=0)
+        total = jnp.sum(jnp.exp(parts - top[None]), axis=0)
+        a.append(standing((top + jnp.log(total) - math.log(G * width * S))[:1, :]))
+    a = jnp.stack(a)
     for j in range(G):
         first, second = BV[j, 0, 0:1, :], BV[j, 1, 0:1, :]
         b = jnp.maximum(first, second) + jnp.log(1.0 + jnp.exp(-jnp.abs(first - second)))
@@ -261,6 +295,7 @@
     width = tgt.shape[0]
     height = n * S
     half = height // 2
+    wide = max(half, 128)
     Z, HF, HR = S // 2, G // 2, (G - 1) // 2
     f32, bf16 = jnp.float32, jnp.bfloat16
     dma = pltpu.SemaphoreType.DMA
@@ -281,19 +316,22 @@
             pltpu.VMEM((G, 2, half, width), f32),
             pltpu.VMEM((2, half, 128), f32),
             pltpu.VMEM((n, 128), f32),
+            pltpu.VMEM((8, wide), f32),
+            pltpu.VMEM((G, 8, wide), f32),
             pltpu.VMEM((2, 8, width), f32),
             pltpu.VMEM((G, 2, 8, width), f32),
-            pltpu.VMEM((8, height), f32),
-            pltpu.VMEM((S, 8, height), f32),
+            pltpu.VMEM((G, 8, wide), f32),
+            pltpu.VMEM((2, Z * G, 8, wide), f32),
             dma((2,)),
             dma((5,)), dma((5,)),
             dma((Z,)), dma((Z,)),
             dma((HF, Z)), dma((HF, Z)),
             dma((HR, Z)), dma((HR, Z)),
             dma((S,)), dma((S,)),
+            dma((G,)), dma((G,)),
             dma((G, 2)), dma((G, 2)),
             dma((G, 2)), dma((G, 2)),
-            dma((S,)), dma((S,)),
+            dma((G, S)), dma((G, S)),
         ],
         compiler_params=pltpu.CompilerParams(
             collective_id=0, has_side_effects=True, vmem_limit_bytes=56 * 2**20

time: 37.7 us -> 38.1 us (1.011)
  Pallas kernels: 35.9 us -> 36.3 us
    pallas_call x1, Pallas kernels: 35.9 us -> 36.3 us  [body(): pl.pallas_call(functools.partial(kernel, G, S), out_shape=jax.ShapeDtypeS...]
where the time goes in v4:
time: 38.1 us; the launch traced here: 38 us
  Pallas kernels  36.3 us (95%)
  local copies, waits for them, and re-layouts  1.67 us (4%)
    pallas_call x1, Pallas kernels, body(): pl.pallas_call(functools.partial(kernel, G, S), out_shape=jax.ShapeDtypeS...  36.3 us
    unnamed x1, local copies, waits for them, and re-layouts  1.67 us

profile of v4, /device:TPU:0, one launch (start us, length us, event | category | flops | bytes accessed | tf_op | source)
XLA Modules:
  0.0 38.0 jit_solution(14065391385213905757)
XLA Ops:
  0.0 36.3 %shard_map.46 = f32[128,512]{1,0:T(8,128)} custom-call(f32[16,1024]{1,0:T(8,128)} %src.1, f32[1,16]{1,0:T(1,128)} %bitcast.2, f32[128,1024]{1,0:T(8,128)} %tgt.1, f32[1,128]{1,0:T(1,128)} %bitcast.3), custom_call_target="tpu_custom_call" | custom-call | flops 536870912 | bytes 1048576 | tf_op jit(solution)/shard_map/pallas_call | solution.py:304
  36.3 1.7 %copy.6 = f32[128,512]{1,0:T(8,128)} copy(f32[128,512]{1,0:T(8,128)} %shard_map.46) | data formatting | bytes 524288

commit v5 on v3

--- a/solution.py
+++ b/solution.py
@@ -43,7 +43,15 @@
     order = [0]
     for r in range(1, HF + 1):
         order += [G - r] if G - r == r else [G - r, r]
-    zs = [z] + [jnp.bitwise_xor(z, k) for k in range(1, Z)]
+    low_half = jnp.where(z < Z // 2, 1, 0)
+    near = low_half * z + (1 - low_half) * (Z - 1 - z)
+    toward = 2 * low_half - 1
+
+    def nearest(k):
+        both = z + toward * ((k + 1) // 2) if k % 2 else z - toward * (k // 2)
+        return jnp.where(k <= 2 * near, both, low_half * k + (1 - low_half) * (Z - 1 - k))
+
+    zs = [z] + [nearest(k) for k in range(1, Z)]
     other = 1 - c
     sib = z * 2 + other
 
@@ -76,8 +84,19 @@
     TI[c] = jnp.broadcast_to(inv_tgt[...], (8, width))
     pl.semaphore_wait(barrier, S - 1 + 2 * (G - 1))
 
-    for k in range(1, Z):
-        send(src, X.at[g, rows(0), :], z_s.at[k], z_r.at[k], (g, zs[k] * 2 + c))
+    late = []
+
+    def along(piece, where, at_z, step, go):
+        cp = pltpu.make_async_remote_copy(
+            piece, where, z_s.at[(step + 1) // 2, at_z], z_r.at[at_z],
+            device_id=(g, lax.rem(z + step + Z, Z) * 2 + c), device_id_type=MESH,
+        )
+        pl.when(go)(cp.start)
+        late.append((go, cp))
+
+    for step in (-1, 1):
+        there = z + step
+        along(src, X.at[g, rows(0), :], z, step, (there >= 0) & (there < Z))
 
     fwd, back = (ahead[1], s), (ahead[G - 1], s)
 
@@ -144,7 +163,7 @@
     finished = 0
     for t in range(Z + HF):
         ready = []
-        for h in range(HF, -1, -1):
+        for h in range(HF + 1):
             k = t - h
             if not 0 <= k < Z:
                 continue
@@ -153,7 +172,9 @@
                 if k == 0:
                     onward(src, where, 0, 0, "own")
                 else:
-                    arrived(where, z_r.at[k])
+                    arrived(where, z_r.at[zs[k]])
+                    along(where, where, zs[k], 1, (zs[k] < z) & (z + 1 < Z))
+                    along(where, where, zs[k], -1, (zs[k] > z) & (z >= 1))
                     onward(where, where, k, 0, "own")
                     ready.append((0, k))
                 continue
@@ -253,6 +274,8 @@
 
     for cp in sends:
         cp.wait_send()
+    for go, cp in late:
+        pl.when(go)(cp.wait_send)
 
 
 def body(src, inv_src, tgt, inv_tgt):
@@ -287,7 +310,7 @@
             pltpu.VMEM((S, 8, height), f32),
             dma((2,)),
             dma((5,)), dma((5,)),
-            dma((Z,)), dma((Z,)),
+            dma((2, Z)), dma((Z,)),
             dma((HF, Z)), dma((HF, Z)),
             dma((HR, Z)), dma((HR, Z)),
             dma((S,)), dma((S,)),

time: 37.7 us -> 35.9 us (0.952)
  Pallas kernels: 35.9 us -> 34.1 us
    pallas_call x1, Pallas kernels: 35.9 us -> 34.1 us  [body(): pl.pallas_call(functools.partial(kernel, G, S), out_shape=jax.ShapeDtypeS...]
where the time goes in v5:
time: 35.9 us; the launch traced here: 35.8 us
  Pallas kernels  34.1 us (95%)
  local copies, waits for them, and re-layouts  1.67 us (5%)
    pallas_call x1, Pallas kernels, body(): pl.pallas_call(functools.partial(kernel, G, S), out_shape=jax.ShapeDtypeS...  34.1 us
    unnamed x1, local copies, waits for them, and re-layouts  1.67 us

profile of v5, /device:TPU:0, one launch (start us, length us, event | category | flops | bytes accessed | tf_op | source)
XLA Modules:
  0.0 35.8 jit_solution(12312709584549449264)
XLA Ops:
  0.0 34.1 %shard_map.46 = f32[128,512]{1,0:T(8,128)} custom-call(f32[16,1024]{1,0:T(8,128)} %src.1, f32[1,16]{1,0:T(1,128)} %bitcast.2, f32[128,1024]{1,0:T(8,128)} %tgt.1, f32[1,128]{1,0:T(1,128)} %bitcast.3), custom_call_target="tpu_custom_call" | custom-call | flops 536870912 | bytes 1048576 | tf_op jit(solution)/shard_map/pallas_call | solution.py:292
  34.1 1.7 %copy.6 = f32[128,512]{1,0:T(8,128)} copy(f32[128,512]{1,0:T(8,128)} %shard_map.46) | data formatting | bytes 524288

commit v6 on v5

--- a/solution.py
+++ b/solution.py
@@ -194,6 +194,13 @@
             )
         if t == 0:
             send(TI.at[c], TI.at[c], t_s.at[4], t_r.at[4], (g, sib))
+        if t == 1:
+            tcopy.wait()
+            scopy.wait()
+            ready.append((0, 0))
+        if 1 <= t <= 4:
+            targets(c, t - 1)
+        if t == 2:
             lane = lax.broadcasted_iota(jnp.int32, (n, n), 1)
             sub = lax.broadcasted_iota(jnp.int32, (n, n), 0)
             column_inv = jnp.sum(
@@ -204,11 +211,6 @@
             IS[c, rows(0), :] = ISM[...]
             for d in range(1, S):
                 send(ISM, IS.at[c, rows(0), :], is_s.at[d], is_r.at[d], (g, lax.rem(s + d, S)))
-            scopy.wait()
-            prepare(0, 0)
-            tcopy.wait()
-            for i in range(4):
-                targets(c, i)
         for r, k in ready:
             prepare(r, k)
         if 1 <= t <= 4:

time: 35.9 us -> 36.2 us (level)
  no operation moved by 1% of the time
where the time goes in v6:
time: 36.2 us; the launch traced here: 36 us
  Pallas kernels  34.3 us (95%)
  local copies, waits for them, and re-layouts  1.67 us (5%)
    pallas_call x1, Pallas kernels, body(): pl.pallas_call(functools.partial(kernel, G, S), out_shape=jax.ShapeDtypeS...  34.3 us
    unnamed x1, local copies, waits for them, and re-layouts  1.67 us

profile of v6, /device:TPU:0, one launch (start us, length us, event | category | flops | bytes accessed | tf_op | source)
XLA Modules:
  0.0 36.0 jit_solution(8231209108635596708)
XLA Ops:
  0.0 34.3 %shard_map.46 = f32[128,512]{1,0:T(8,128)} custom-call(f32[16,1024]{1,0:T(8,128)} %src.1, f32[1,16]{1,0:T(1,128)} %bitcast.2, f32[128,1024]{1,0:T(8,128)} %tgt.1, f32[1,128]{1,0:T(1,128)} %bitcast.3), custom_call_target="tpu_custom_call" | custom-call | flops 536870912 | bytes 1048576 | tf_op jit(solution)/shard_map/pallas_call | solution.py:294
  34.4 1.7 %copy.6 = f32[128,512]{1,0:T(8,128)} copy(f32[128,512]{1,0:T(8,128)} %shard_map.46) | data formatting | bytes 524288
